TPU v7x, 32 devices: a whole 2x2x4 slice. The times are simulated.
32 devices in a mesh: step: 4 (over y, x), frame: 8 (over z, core).
Axes of the slice: x: 2, y: 2, z: 4, core: 2. Of those that a mesh axis runs over, the one named last changes fastest.
Arguments:
- start_state: bfloat16 [8, 32, 32, 320], P('frame'), may hold values from -6 to 6
- step_noise: bfloat16 [4, 8, 32, 32, 320], P('step', 'frame'), may hold values from -6 to 6
- timesteps: int32 [4], P('step'), may hold values from 0 to 999
- gn_gain: float32 [320], replicated, may hold values from 0.1 to 1.9
- gn_bias: float32 [320], replicated, may hold values from -3 to 3
- spatial_weight: bfloat16 [3, 3, 320, 320], replicated, may hold values from -0.109375 to 0.109375
- temporal_weight: bfloat16 [3, 320, 320], replicated, may hold values from -0.1875 to 0.1875
- temb_weight: bfloat16 [320, 320], replicated, may hold values from -0.3125 to 0.3125
Outputs:
- next_states: bfloat16 [4, 8, 32, 32, 320], P('step', 'frame')
All inputs are finite; a program needn't handle non-finite values.
Results may differ from a plain program's by a relative error of at most 0.005.
Values may be sent and summed in bfloat16 or wider, within the bound.
A program may use at most 128 MiB of HBM per device.

v0:
```python
import math

import jax
import jax.numpy as jnp
from jax import lax
from jax.sharding import PartitionSpec as P

GROUPS = 32


def extended_2(cells, sides, width):
    for axis, dim in sides:
        count = lax.axis_size(axis)
        ends = count - 1
        head = lax.slice_in_dim(cells, 0, width, axis=dim)
        tail = lax.slice_in_dim(cells, cells.shape[dim] - width, cells.shape[dim], axis=dim)
        cells = jnp.concatenate(
            [
                lax.ppermute(tail, axis, [(i, (i + 1) % count) for i in range(ends)]),
                cells,
                lax.ppermute(head, axis, [((i + 1) % count, i) for i in range(ends)]),
            ],
            axis=dim,
        )
    return cells


def entering(part, axis, combine, identity):
    place = lax.axis_index(axis)
    gathered = lax.all_gather(part, axis)
    state = jnp.zeros_like(part) + jnp.asarray(identity, part.dtype)

    def one(hop, state):
        return combine(state, lax.dynamic_index_in_dim(gathered, hop, 0, False))

    return lax.fori_loop(0, place, one, state)


def norm_silu(current, gn_gain, gn_bias):
    frames_here, rows, columns, channels = current.shape
    grouped = current.astype(jnp.float32).reshape(
        frames_here, rows, columns, GROUPS, channels // GROUPS
    )
    group_mean = jnp.mean(grouped, axis=(1, 2, 4), keepdims=True)
    centered = grouped - group_mean
    group_var = jnp.mean(centered * centered, axis=(1, 2, 4), keepdims=True)
    scaled = (centered * lax.rsqrt(group_var + 1e-05)).reshape(frames_here, rows, columns, channels)
    return jax.nn.silu(scaled * gn_gain + gn_bias).astype(jnp.bfloat16)


def time_vector(step_index, temb_weight):
    half_dim = temb_weight.shape[0] // 2
    frequencies = jnp.exp(-math.log(10000.0) * jnp.arange(half_dim, dtype=jnp.float32) / half_dim)
    angles = step_index.astype(jnp.float32) * frequencies
    embedding = jnp.concatenate([jnp.cos(angles), jnp.sin(angles)]).astype(jnp.bfloat16)
    return jax.nn.silu(jnp.dot(embedding, temb_weight, preferred_element_type=jnp.float32))


def spatial_conv(normed, spatial_weight):
    rows, columns = (normed.shape[1], normed.shape[2])
    padded = jnp.pad(normed, ((0, 0), (1, 1), (1, 1), (0, 0)))
    total = None
    for row_off in range(3):
        for col_off in range(3):
            window = padded[:, row_off : row_off + rows, col_off : col_off + columns, :]
            term = jnp.dot(
                window, spatial_weight[row_off, col_off], preferred_element_type=jnp.float32
            )
            total = term if total is None else total + term
    return total


def frame_conv(extended, temporal_weight, frames_out):
    total = None
    for offset in range(3):
        term = jnp.dot(
            extended[offset : offset + frames_out],
            temporal_weight[offset],
            preferred_element_type=jnp.float32,
        )
        total = term if total is None else total + term
    return total.astype(jnp.bfloat16)


def combine_sum(earlier, later):
    return earlier + later


def local(
    start_state,
    step_noise,
    timesteps,
    gn_gain,
    gn_bias,
    spatial_weight,
    temporal_weight,
    temb_weight,
):
    time_bias = time_vector(timesteps[0], temb_weight)
    noise_wide = step_noise[0].astype(jnp.float32)
    start_wide = start_state.astype(jnp.float32)
    current = start_state
    result = start_state
    for sweep_index in range(2):
        normed = norm_silu(current, gn_gain, gn_bias)
        drift_activated = jax.nn.silu(spatial_conv(normed, spatial_weight) + time_bias).astype(
            jnp.bfloat16
        )
        extended = extended_2(drift_activated, (("frame", 0),), 1)
        update = frame_conv(extended, temporal_weight, drift_activated.shape[0])
        drift_now = 0.25 * update.astype(jnp.float32) + 0.25 * noise_wide
        earlier_sum = entering(drift_now, "step", combine_sum, jnp.zeros_like(drift_now))
        baseline = start_wide + earlier_sum
        if sweep_index == 0:
            current = baseline.astype(jnp.bfloat16)
        else:
            result = (baseline + drift_now).astype(jnp.bfloat16)
    return result[None]


def solution(mesh):
    placed = (
        P("frame", None, None, None),
        P("step", "frame", None, None, None),
        P("step"),
        P(),
        P(),
        P(),
        P(),
        P(),
    )
    return jax.shard_map(
        local,
        mesh=mesh,
        in_specs=placed,
        out_specs=P("step", "frame", None, None, None),
        check_vma=False,
    )
```

profile of v0, /device:TPU:23, one launch (start us, length us, event | category | flops | bytes accessed | tf_op | source)
XLA Modules:
  0.0 226.5 jit_solution(2994310618158257595)
XLA Ops:
  6.6 1.5 convert_reduce_fusion
  8.1 0.1 reduce_sum.47
  8.2 0.1 reduce_sum.51
  8.4 0.1 sub.37
  8.5 1.4 fusion.4
  9.9 0.1 reduce_sum.53
  10.0 0.1 reduce_sum.54
  10.2 0.1 mul.111
  10.3 0.6 fusion.12
  10.9 0.6 fusion.26
  11.5 0.6 fusion.29
  12.2 0.6 fusion.32
  12.8 0.6 fusion.35
  13.4 0.6 fusion.38
  14.1 0.6 fusion.41
  14.7 0.6 fusion.44
  15.3 0.6 fusion.86
  16.7 0.2 convolution_reduce_fusion
  16.9 1.2 multiply_convert_fusion.1
  18.1 3.8 %collective-permute-start = (bf16[1,32,32,320]{3,2,1,0:T(8,128)(2,1)S(1)}, bf16[1,32,32,320]{3,2,1,0:T(8,128)(2,1)S(1)}, u32[]{:S(2)}, u32[]{:S(2)}) collective-permute-start(bf16[1,32,32,320]{3,2,1,0:T(8,128)(2,1)S(1)} %bitcast.185), channel_id=1, source_target_pairs={{0,1},{1,2},{2,3},{3,4},{4,5},{5,6},{6,7},{8,9},{9,10},{10,11},{11... | collective-permute-start | bytes 1966088 | tf_op jit(solution)/shard_map/ppermute | solution.py:19
  21.9 1.9 collective-permute-start.1
  23.8 0.6 fusion.110
  24.5 6.3 %collective-permute-done = bf16[1,32,32,320]{3,2,1,0:T(8,128)(2,1)S(1)} collective-permute-done((bf16[1,32,32,320]{3,2,1,0:T(8,128)(2,1)S(1)}, bf16[1,32,32,320]{3,2,1,0:T(8,128)(2,1)S(1)}, u32[]{:S(2)}, u32[]{:S(2)}) %collective-permute-start) | collective-permute-done | bytes 655392 | tf_op jit(solution)/shard_map/ppermute | solution.py:19
  30.8 0.6 fusion.84
  31.4 3.8 %collective-permute-done.1 = bf16[1,32,32,320]{3,2,1,0:T(8,128)(2,1)S(1)} collective-permute-done((bf16[1,32,32,320]{3,2,1,0:T(8,128)(2,1)S(1)}, bf16[1,32,32,320]{3,2,1,0:T(8,128)(2,1)S(1)}, u32[]{:S(2)}, u32[]{:S(2)}) %collective-permute-start.1) | collective-permute-done | bytes 655392 | tf_op jit(solution)/shard_map/ppermute | solution.py:21
  35.2 1.9 bitcast_add_fusion.3
  37.2 68.8 %all-gather.5.cloned.1.call-done = f32[128,32,320]{2,1,0:T(8,128)} async-done(((f32[32,32,320]{2,1,0:T(8,128)}), f32[128,32,320]{2,1,0:T(8,128)}) %all-gather.5.cloned.1.call-update) | async-done | bytes 5242896 | tf_op jit(solution)/shard_map/all_gather | solution.py:30
  106.0 0.2 broadcast.124.clone
  106.2 5.7 %while.20 = (s32[]{:T(128)}, f32[1,32,32,320]{3,2,1,0:T(8,128)S(1)}, s32[]{:T(128)}, f32[4,1,32,32,320]{4,3,2,1,0:T(8,128)}, s32[]{:T(128)}, /*index=5*/s32[]{:T(128)}, s32[]{:T(128)}) while((s32[]{:T(128)}, f32[1,32,32,320]{3,2,1,0:T(8,128)S(1)}, s32[]{:T(128)}, f32[4,1,32,32,320]{4,3,2,1,0:T(8,128)}, s32[]{:T(128)}, /*index=5*/s32[]{:T(128)}, ...), condition=%wide.region_5.6_spmd, body=%wide.region_4.5_spmd.sunk | while | flops 327685 | bytes 3932275 | solution.py:36
  106.2 1.8 bitcast_add_fusion.6
  108.1 1.8 bitcast_add_fusion.6
  109.9 1.8 bitcast_add_fusion.6
  111.9 1.1 convert_reduce_fusion.1
  113.1 0.1 reduce_sum.59
  113.2 0.1 reduce_sum.72
  113.4 0.1 sub.41
  113.5 1.6 fusion.13
  115.1 0.1 reduce_sum.74
  115.2 0.1 reduce_sum.75
  115.4 0.1 mul.126
  115.5 1.7 fusion.21
  117.2 0.6 fusion.49
  117.9 0.6 fusion.52
  118.5 0.6 fusion.55
  119.1 0.6 fusion.58
  119.8 0.6 fusion.61
  120.4 0.6 fusion.64
  121.0 0.6 fusion.67
  121.7 0.6 fusion.78
  122.3 1.2 multiply_convert_fusion
  123.5 3.7 %collective-permute-start.2 = (bf16[1,32,32,320]{3,2,1,0:T(8,128)(2,1)S(1)}, bf16[1,32,32,320]{3,2,1,0:T(8,128)(2,1)S(1)}, u32[]{:S(2)}, u32[]{:S(2)}) collective-permute-start(bf16[1,32,32,320]{3,2,1,0:T(8,128)(2,1)S(1)} %bitcast.183), channel_id=1, source_target_pairs={{0,1},{1,2},{2,3},{3,4},{4,5},{5,6},{6,7},{8,9},{9,10},{10,11},{11... | collective-permute-start | bytes 1966088 | tf_op jit(solution)/shard_map/ppermute | solution.py:19
  127.1 1.9 collective-permute-start.3
  129.1 0.6 fusion.108
  129.7 6.3 %collective-permute-done.2 = bf16[1,32,32,320]{3,2,1,0:T(8,128)(2,1)S(1)} collective-permute-done((bf16[1,32,32,320]{3,2,1,0:T(8,128)(2,1)S(1)}, bf16[1,32,32,320]{3,2,1,0:T(8,128)(2,1)S(1)}, u32[]{:S(2)}, u32[]{:S(2)}) %collective-permute-start.2) | collective-permute-done | bytes 655392 | tf_op jit(solution)/shard_map/ppermute | solution.py:19
  136.0 0.6 fusion.76
  136.7 3.8 %collective-permute-done.3 = bf16[1,32,32,320]{3,2,1,0:T(8,128)(2,1)S(1)} collective-permute-done((bf16[1,32,32,320]{3,2,1,0:T(8,128)(2,1)S(1)}, bf16[1,32,32,320]{3,2,1,0:T(8,128)(2,1)S(1)}, u32[]{:S(2)}, u32[]{:S(2)}) %collective-permute-start.3) | collective-permute-done | bytes 655392 | tf_op jit(solution)/shard_map/ppermute | solution.py:21
  140.4 1.9 bitcast_add_fusion.2
  142.4 68.9 %all-gather.7.cloned.1.call-done = f32[128,32,320]{2,1,0:T(8,128)} async-done(((f32[32,32,320]{2,1,0:T(8,128)}), f32[128,32,320]{2,1,0:T(8,128)}) %all-gather.7.cloned.1.call-update) | async-done | bytes 5242896 | tf_op jit(solution)/shard_map/all_gather | solution.py:30
  211.3 0.2 broadcast.124
  211.5 5.5 %while.21 = (s32[]{:T(128)}, f32[1,32,32,320]{3,2,1,0:T(8,128)S(1)}, s32[]{:T(128)}, f32[4,1,32,32,320]{4,3,2,1,0:T(8,128)}, s32[]{:T(128)}, /*index=5*/s32[]{:T(128)}, s32[]{:T(128)}) while((s32[]{:T(128)}, f32[1,32,32,320]{3,2,1,0:T(8,128)S(1)}, s32[]{:T(128)}, f32[4,1,32,32,320]{4,3,2,1,0:T(8,128)}, s32[]{:T(128)}, ...), condition=%wide.region_11.12_spmd, body=%wide.region_10.11_spmd.sunk | while | flops 327685 | bytes 3932275 | solution.py:36
  211.5 1.8 bitcast_add_fusion.7
  213.3 1.8 bitcast_add_fusion.7
  215.2 1.8 bitcast_add_fusion.7
  217.0 2.7 %fusion.71 = bf16[1,1,32,32,320]{4,3,2,1,0:T(8,128)(2,1)} fusion(f32[32,32,320]{2,1,0:T(8,128)} %bitcast_add_fusion.2, f32[1,32,32,320]{3,2,1,0:T(8,128)S(1)} %get-tuple-element.52, bf16[1,32,32,320]{3,2,1,0:T(8,128)(2,1)S(1)} %copy-done.1), kind=kLoop, calls=%fused_computation.87 | loop fusion | flops 1310720 | bytes 3932160 | tf_op jit(solution)/shard_map/broadcast_in_dim | solution.py:118
  (36 shorter events, 0.6 us)
Async XLA Ops:
  6.5 10.2 %copy-start = (bf16[320,320]{1,0:T(8,128)(2,1)S(1)}, bf16[320,320]{1,0:T(8,128)(2,1)}, u32[]{:S(2)}) copy-start(bf16[320,320]{1,0:T(8,128)(2,1)} %param.19) | copy-start | bytes 614404
  6.5 3.8 %copy-start.1 = (bf16[1,32,32,320]{3,2,1,0:T(8,128)(2,1)S(1)}, bf16[1,32,32,320]{3,2,1,0:T(8,128)(2,1)}, u32[]{:S(2)}) copy-start(bf16[1,32,32,320]{3,2,1,0:T(8,128)(2,1)} %param.12) | copy-start | bytes 1966084
  6.5 3.8 %copy-start.9 = (f32[320]{0:T(512)S(1)}, f32[320]{0:T(512)}, u32[]{:S(2)}) copy-start(f32[320]{0:T(512)} %param.15) | copy-start | bytes 3844
  6.5 3.8 %copy-start.8 = (f32[320]{0:T(512)S(1)}, f32[320]{0:T(512)}, u32[]{:S(2)}) copy-start(f32[320]{0:T(512)} %param.16) | copy-start | bytes 3844
  6.5 4.4 %copy-start.2 = (bf16[3,3,320,320]{3,2,1,0:T(8,128)(2,1)S(1)}, bf16[3,3,320,320]{3,2,1,0:T(8,128)(2,1)}, u32[]{:S(2)}) copy-start(bf16[3,3,320,320]{3,2,1,0:T(8,128)(2,1)} %param.17) | copy-start | bytes 5529604
  6.6 99.5 %all-gather.5.cloned.1.call-start = ((), (), s32[]{:S(2)}) async-start(), calls=%async_computation | async-start | bytes 7864320 | tf_op jit(solution)/shard_map/all_gather | solution.py:30
  16.9 6.9 %copy-start.6 = (bf16[3,320,320]{2,1,0:T(8,128)(2,1)S(1)}, bf16[3,320,320]{2,1,0:T(8,128)(2,1)}, u32[]{:S(2)}) copy-start(bf16[3,320,320]{2,1,0:T(8,128)(2,1)} %param.18) | copy-start | bytes 1843204
  18.1 12.7 %collective-permute-start = (bf16[1,32,32,320]{3,2,1,0:T(8,128)(2,1)S(1)}, bf16[1,32,32,320]{3,2,1,0:T(8,128)(2,1)S(1)}, u32[]{:S(2)}, u32[]{:S(2)}) collective-permute-start(bf16[1,32,32,320]{3,2,1,0:T(8,128)(2,1)S(1)} %bitcast.185), channel_id=1, source_target_pairs={{0,1},{1,2},{2,3},{3,4},{4,5},{5,6},{6,7},{8,9},{9,10},{10,11},{11... | collective-permute-start | bytes 1966088 | tf_op jit(solution)/shard_map/ppermute | solution.py:19
  21.9 13.3 %collective-permute-start.1 = (bf16[1,32,32,320]{3,2,1,0:T(8,128)(2,1)S(1)}, bf16[1,32,32,320]{3,2,1,0:T(8,128)(2,1)S(1)}, u32[]{:S(2)}, u32[]{:S(2)}) collective-permute-start(bf16[1,32,32,320]{3,2,1,0:T(8,128)(2,1)S(1)} %bitcast.186), channel_id=1, source_target_pairs={{1,0},{2,1},{3,2},{4,3},{5,4},{6,5},{7,6},{9,8},{10,9},{11,10},{12... | collective-permute-start | bytes 1966088 | tf_op jit(solution)/shard_map/ppermute | solution.py:21
  24.4 10.7 %copy-start.4 = (bf16[1,1,32,32,320]{4,3,2,1,0:T(8,128)(2,1)S(1)}, bf16[1,1,32,32,320]{4,3,2,1,0:T(8,128)(2,1)}, u32[]{:S(2)}) copy-start(bf16[1,1,32,32,320]{4,3,2,1,0:T(8,128)(2,1)} %param.13) | copy-start | bytes 1966084
  37.2 174.1 %all-gather.7.cloned.1.call-start = ((), (), s32[]{:S(2)}) async-start(), calls=%async_computation.1 | async-start | bytes 7864320 | tf_op jit(solution)/shard_map/all_gather | solution.py:30
  113.1 4.2 %copy-start.3 = (bf16[3,3,320,320]{3,2,1,0:T(8,128)(2,1)S(1)}, bf16[3,3,320,320]{3,2,1,0:T(8,128)(2,1)}, u32[]{:S(2)}) copy-start(bf16[3,3,320,320]{3,2,1,0:T(8,128)(2,1)} %param.17) | copy-start | bytes 5529604
  122.3 6.8 %copy-start.7 = (bf16[3,320,320]{2,1,0:T(8,128)(2,1)S(1)}, bf16[3,320,320]{2,1,0:T(8,128)(2,1)}, u32[]{:S(2)}) copy-start(bf16[3,320,320]{2,1,0:T(8,128)(2,1)} %param.18) | copy-start | bytes 1843204
  123.5 12.6 %collective-permute-start.2 = (bf16[1,32,32,320]{3,2,1,0:T(8,128)(2,1)S(1)}, bf16[1,32,32,320]{3,2,1,0:T(8,128)(2,1)S(1)}, u32[]{:S(2)}, u32[]{:S(2)}) collective-permute-start(bf16[1,32,32,320]{3,2,1,0:T(8,128)(2,1)S(1)} %bitcast.183), channel_id=1, source_target_pairs={{0,1},{1,2},{2,3},{3,4},{4,5},{5,6},{6,7},{8,9},{9,10},{10,11},{11... | collective-permute-start | bytes 1966088 | tf_op jit(solution)/shard_map/ppermute | solution.py:19
  127.1 13.3 %collective-permute-start.3 = (bf16[1,32,32,320]{3,2,1,0:T(8,128)(2,1)S(1)}, bf16[1,32,32,320]{3,2,1,0:T(8,128)(2,1)S(1)}, u32[]{:S(2)}, u32[]{:S(2)}) collective-permute-start(bf16[1,32,32,320]{3,2,1,0:T(8,128)(2,1)S(1)} %bitcast.184), channel_id=1, source_target_pairs={{1,0},{2,1},{3,2},{4,3},{5,4},{6,5},{7,6},{9,8},{10,9},{11,10},{12... | collective-permute-start | bytes 1966088 | tf_op jit(solution)/shard_map/ppermute | solution.py:21
  129.7 10.7 %copy-start.5 = (bf16[1,1,32,32,320]{4,3,2,1,0:T(8,128)(2,1)S(1)}, bf16[1,1,32,32,320]{4,3,2,1,0:T(8,128)(2,1)}, u32[]{:S(2)}) copy-start(bf16[1,1,32,32,320]{4,3,2,1,0:T(8,128)(2,1)} %param.13) | copy-start | bytes 1966084
Sparse Core Ops, SparseCore 0:
  37.3 68.6 all-gather.4
  142.5 68.6 all-gather.6
where the time goes:
time: 227 us
  waiting for transfers between devices  158 us (70%)
  other arithmetic  22.1 us (10%)
  matrix products  18.8 us (8%)
  between operations  14.5 us (6%)
  starting transfers between devices  11.4 us (5%)
    all_gather x2, waiting for transfers between devices, entering(): gathered = lax.all_gather(part, axis)  138 us
    ppermute x2, waiting for transfers between devices, extended_2(): lax.ppermute(tail, axis, [(i, (i + 1) % count) for i in range(ends)])  12.7 us
    dot_general x18, matrix products, spatial_conv(): jnp.dot(window, spatial_weight[row_off, col_off], preferred_element_type=...  12.3 us
    add x6, other arithmetic, combine_sum(): return earlier + later  10.9 us
    ppermute x2, waiting for transfers between devices, extended_2(): lax.ppermute(head, axis, [((i + 1) % count, i) for i in range(ends)])  7.54 us
    ppermute x2, starting transfers between devices, extended_2(): lax.ppermute(tail, axis, [(i, (i + 1) % count) for i in range(ends)])  7.43 us
    dot_general x6, matrix products, frame_conv(): jnp.dot(extended[offset:offset + frames_out], temporal_weight[offset], pr...  6.37 us
  transfers between devices with their start and end apart: 6, of which 6 were waited for; matrix products, arithmetic and copies ran while one was open for 1% of the time, Pallas kernels for 0%

commit v1 on v0

--- a/solution.py
+++ b/solution.py
@@ -25,15 +25,20 @@
     return cells
 
 
-def entering(part, axis, combine, identity):
+def prefix(part, axis):
+    count = lax.axis_size(axis)
     place = lax.axis_index(axis)
-    gathered = lax.all_gather(part, axis)
-    state = jnp.zeros_like(part) + jnp.asarray(identity, part.dtype)
-
-    def one(hop, state):
-        return combine(state, lax.dynamic_index_in_dim(gathered, hop, 0, False))
-
-    return lax.fori_loop(0, place, one, state)
+    wide = part.astype(jnp.float32)
+    before = jnp.zeros_like(wide)
+    total = wide
+    hop = 1
+    while hop < count:
+        pairs = [(i, i ^ hop) for i in range(count) if 2 * hop < count or not i & hop]
+        got = lax.ppermute(total.astype(jnp.bfloat16), axis, pairs).astype(jnp.float32)
+        before = before + jnp.where((place & hop) != 0, got, 0.0)
+        total = total + got
+        hop *= 2
+    return before
 
 
 def norm_silu(current, gn_gain, gn_bias):
@@ -82,10 +87,6 @@
     return total.astype(jnp.bfloat16)
 
 
-def combine_sum(earlier, later):
-    return earlier + later
-
-
 def local(
     start_state,
     step_noise,
@@ -96,25 +97,26 @@
     temporal_weight,
     temb_weight,
 ):
-    time_bias = time_vector(timesteps[0], temb_weight)
-    noise_wide = step_noise[0].astype(jnp.float32)
+    place = lax.axis_index("step")
+    count = lax.axis_size("step")
+    steps = lax.all_gather(timesteps[0], "step")
+    biases = [time_vector(steps[s], temb_weight) for s in range(count)]
+    own_bias = time_vector(timesteps[0], temb_weight)
+    noise_before = prefix(step_noise[0], "step")
     start_wide = start_state.astype(jnp.float32)
-    current = start_state
-    result = start_state
-    for sweep_index in range(2):
-        normed = norm_silu(current, gn_gain, gn_bias)
-        drift_activated = jax.nn.silu(spatial_conv(normed, spatial_weight) + time_bias).astype(
-            jnp.bfloat16
-        )
-        extended = extended_2(drift_activated, (("frame", 0),), 1)
-        update = frame_conv(extended, temporal_weight, drift_activated.shape[0])
-        drift_now = 0.25 * update.astype(jnp.float32) + 0.25 * noise_wide
-        earlier_sum = entering(drift_now, "step", combine_sum, jnp.zeros_like(drift_now))
-        baseline = start_wide + earlier_sum
-        if sweep_index == 0:
-            current = baseline.astype(jnp.bfloat16)
-        else:
-            result = (baseline + drift_now).astype(jnp.bfloat16)
+    conv = spatial_conv(norm_silu(start_state, gn_gain, gn_bias), spatial_weight)
+    activated = jnp.zeros_like(conv)
+    for s in range(count - 1):
+        activated += jnp.where(s < place, jax.nn.silu(conv + biases[s]), 0.0)
+    extended = extended_2(activated.astype(jnp.bfloat16), (("frame", 0),), 1)
+    update = frame_conv(extended, temporal_weight, 1).astype(jnp.float32)
+    current = (start_wide + 0.25 * (update + noise_before)).astype(jnp.bfloat16)
+    conv = spatial_conv(norm_silu(current, gn_gain, gn_bias), spatial_weight)
+    activated = jax.nn.silu(conv + own_bias).astype(jnp.bfloat16)
+    extended = extended_2(activated, (("frame", 0),), 1)
+    update = frame_conv(extended, temporal_weight, 1)
+    drift = update.astype(jnp.float32) + step_noise[0].astype(jnp.float32)
+    result = (start_wide + 0.25 * (noise_before + drift + prefix(update, "step"))).astype(jnp.bfloat16)
     return result[None]
 
 

time: 227 us -> 141 us (0.62)
  waiting for transfers between devices: 158 us -> 62.8 us
  matrix products: 18.8 us -> 38.8 us
  other arithmetic: 22.1 us -> 8.27 us
  between operations: 14.5 us -> 3.09 us
  starting transfers between devices: 11.4 us -> 18.6 us
  blocking collectives: 0 us -> 4.34 us
    all_gather x2 -> x0, waiting for transfers between devices: 138 us -> none  [entering(): gathered = lax.all_gather(part, axis)]
    ppermute x0 -> x4, waiting for transfers between devices: none -> 47.2 us  [prefix(): lax.ppermute(total.astype(jnp.bfloat16), axis, pairs).astype(jnp.float32)]
    dot_general x18, matrix products: 12.3 us -> 30.1 us  [spatial_conv(): jnp.dot(window, spatial_weight[row_off, col_off], preferred_element_type=...]
    add x6 -> x0, other arithmetic: 10.9 us -> none  [combine_sum(): return earlier + later]
    unnamed x0 -> x1, blocking collectives: none -> 4.34 us
    ppermute x0 -> x4, starting transfers between devices: none -> 4.34 us  [prefix(): lax.ppermute(total.astype(jnp.bfloat16), axis, pairs).astype(jnp.float32)]
    ppermute x2, waiting for transfers between devices: 12.7 us -> 8.97 us  [extended_2(): lax.ppermute(tail, axis, [(i, (i + 1) % count) for i in range(ends)])]
    ppermute x2, starting transfers between devices: 7.43 us -> 10.4 us  [extended_2(): lax.ppermute(tail, axis, [(i, (i + 1) % count) for i in range(ends)])]
  transfers between devices with their start and end apart: 6 -> 8, of which waited for: 6 -> 7; matrix products, arithmetic and copies ran while one was open for 1% -> 26% of each run, Pallas kernels for 0% -> 0%
where the time goes in v1:
time: 141 us; the launch traced here: 139 us
  waiting for transfers between devices  62.8 us (45%)
  matrix products  38.8 us (28%)
  starting transfers between devices  18.6 us (13%)
  other arithmetic  8.27 us (6%)
  blocking collectives  4.34 us (3%)
  local copies, waits for them, and re-layouts  3.24 us (2%)
  between operations  3.09 us (2%)
    ppermute x4, waiting for transfers between devices, prefix(): lax.ppermute(total.astype(jnp.bfloat16), axis, pairs).astype(jnp.float32)  47.2 us
    dot_general x18, matrix products, spatial_conv(): jnp.dot(window, spatial_weight[row_off, col_off], preferred_element_type=...  30.1 us
    ppermute x2, starting transfers between devices, extended_2(): lax.ppermute(tail, axis, [(i, (i + 1) % count) for i in range(ends)])  10.4 us
    ppermute x2, waiting for transfers between devices, extended_2(): lax.ppermute(tail, axis, [(i, (i + 1) % count) for i in range(ends)])  8.97 us
    dot_general x6, matrix products, frame_conv(): jnp.dot(extended[offset:offset + frames_out], temporal_weight[offset], pr...  7.97 us
    ppermute x2, waiting for transfers between devices, extended_2(): lax.ppermute(head, axis, [((i + 1) % count, i) for i in range(ends)])  6.6 us
    unnamed x1, blocking collectives  4.34 us
    ppermute x4, starting transfers between devices, prefix(): lax.ppermute(total.astype(jnp.bfloat16), axis, pairs).astype(jnp.float32)  4.34 us
  transfers between devices with their start and end apart: 8, of which 7 were waited for; matrix products, arithmetic and copies ran while one was open for 26% of the time, Pallas kernels for 0%

profile of v1, /device:TPU:23, one launch (start us, length us, event | category | flops | bytes accessed | tf_op | source)
XLA Modules:
  0.0 139.1 jit_solution(17940911546512391353)
XLA Ops:
  0.0 0.3 collective-permute-start
  0.3 1.3 convert_reduce_fusion
  1.8 0.1 reduce_sum.51
  2.0 0.1 sub.37
  2.1 1.4 %fusion.4 = f32[320]{0:T(512)S(1)} fusion(bf16[1,32,32,320]{3,2,1,0:T(8,128)(2,1)} %param.8, f32[320]{0:T(512)S(1)} %sub.37), kind=kLoop, calls=%fused_computation.16 | loop fusion | flops 1310400 | bytes 657920 | tf_op jit(solution)/shard_map/reduce_sum | solution.py:51
  3.6 0.1 reduce_sum.54
  3.8 0.1 mul.138
  3.9 0.6 fusion.12
  4.5 2.9 %fusion.34 = f32[32,32,320]{2,1,0:T(8,128)} fusion(bf16[1,32,32,320]{3,2,1,0:T(8,128)(2,1)S(1)} %fusion.12, bf16[3,3,320,320]{3,2,1,0:T(8,128)(2,1)} %param.13), kind=kOutput, calls=%fused_computation.71 | convolution fusion | flops 209715200 | bytes 2211840 | tf_op jit(solution)/shard_map/dot_general | solution.py:71
  7.4 1.8 %fusion.37 = f32[32,32,320]{2,1,0:T(8,128)} fusion(bf16[1,32,32,320]{3,2,1,0:T(8,128)(2,1)S(1)} %fusion.12, bf16[3,3,320,320]{3,2,1,0:T(8,128)(2,1)S(1)} %copy-done.2), kind=kOutput, calls=%fused_computation.73 | convolution fusion | flops 209715200 | bytes 2342912 | tf_op jit(solution)/shard_map/dot_general | solution.py:71
  9.2 1.9 %fusion.40 = f32[32,32,320]{2,1,0:T(8,128)} fusion(bf16[1,32,32,320]{3,2,1,0:T(8,128)(2,1)S(1)} %fusion.12, bf16[3,3,320,320]{3,2,1,0:T(8,128)(2,1)S(1)} %copy-done.2), kind=kOutput, calls=%fused_computation.75 | convolution fusion | flops 209715200 | bytes 2342912 | tf_op jit(solution)/shard_map/dot_general | solution.py:71
  11.0 1.8 %fusion.43 = f32[32,32,320]{2,1,0:T(8,128)} fusion(bf16[1,32,32,320]{3,2,1,0:T(8,128)(2,1)S(1)} %fusion.12, bf16[3,3,320,320]{3,2,1,0:T(8,128)(2,1)S(1)} %copy-done.2), kind=kOutput, calls=%fused_computation.77 | convolution fusion | flops 209715200 | bytes 2342912 | tf_op jit(solution)/shard_map/dot_general | solution.py:71
  12.8 1.8 %fusion.46 = f32[32,32,320]{2,1,0:T(8,128)} fusion(bf16[1,32,32,320]{3,2,1,0:T(8,128)(2,1)S(1)} %fusion.12, bf16[3,3,320,320]{3,2,1,0:T(8,128)(2,1)S(1)} %copy-done.2), kind=kOutput, calls=%fused_computation.79 | convolution fusion | flops 209715200 | bytes 2342912 | tf_op jit(solution)/shard_map/dot_general | solution.py:71
  14.5 1.8 %fusion.49 = f32[32,32,320]{2,1,0:T(8,128)} fusion(bf16[1,32,32,320]{3,2,1,0:T(8,128)(2,1)S(1)} %fusion.12, bf16[3,3,320,320]{3,2,1,0:T(8,128)(2,1)S(1)} %copy-done.2), kind=kOutput, calls=%fused_computation.81 | convolution fusion | flops 209715200 | bytes 2342912 | tf_op jit(solution)/shard_map/dot_general | solution.py:71
  16.3 1.8 %fusion.94 = f32[32,32,320]{2,1,0:T(8,128)} fusion(bf16[1,32,32,320]{3,2,1,0:T(8,128)(2,1)S(1)} %fusion.12, bf16[3,3,320,320]{3,2,1,0:T(8,128)(2,1)S(1)} %copy-done.2), kind=kOutput, calls=%fused_computation.111 | convolution fusion | flops 209715200 | bytes 2342912 | tf_op jit(solution)/shard_map/dot_general | solution.py:71
  18.8 0.6 dynamic-slice
  19.4 0.8 dynamic-update-slice
  20.1 2.7 %fusion.52 = f32[32,32,320]{2,1,0:T(8,128)} fusion(bf16[1,32,32,320]{3,2,1,0:T(8,128)(2,1)S(1)} %fusion.12, bf16[3,3,320,320]{3,2,1,0:T(8,128)(2,1)} %param.13), kind=kOutput, calls=%fused_computation.83 | convolution fusion | flops 209715200 | bytes 2211840 | tf_op jit(solution)/shard_map/dot_general | solution.py:71
  22.8 4.3 %all-reduce.2 = s32[4]{0:T(128)S(1)} all-reduce(s32[4]{0:T(128)S(1)} %dynamic-update-slice), channel_id=1, replica_groups=mesh['step'=4,'frame'=8] {'step'}, use_global_device_ids=true, to_apply=%add.2 | all-reduce | flops 4 | bytes 32
  27.2 0.7 fusion.167
  28.7 0.2 convolution_reduce_fusion.1
  29.6 0.2 convolution_reduce_fusion.2
  30.6 0.2 convolution_reduce_fusion.3
  30.8 6.6 %add_convert_fusion.2 = bf16[32,32,320]{2,1,0:T(8,128)(2,1)} fusion(f32[32,32,320]{2,1,0:T(8,128)} %fusion.52, f32[32,32,320]{2,1,0:T(8,128)} %fusion.49, f32[32,32,320]{2,1,0:T(8,128)} %fusion.46, f32[32,32,320]{2,1,0:T(8,128)} %fusion.94, f32[32,32,320]{2,1,0:T(8,128)} %fusion.43, f32[32,32,320]{2,1,0:T(8,128)} %fusion.40, f32[32,32,320]{2,1,0:T(8,128)} %fusion.34, ...), kind=kOutput, calls=%fused_computation.49 | convolution fusion | flops 219217920 | bytes 14143235 | tf_op jit(solution)/shard_map/dot_general | solution.py:71
  37.4 6.2 %collective-permute-start.2 = (bf16[1,32,32,320]{3,2,1,0:T(8,128)(2,1)}, bf16[1,32,32,320]{3,2,1,0:T(8,128)(2,1)}, u32[]{:S(2)}, u32[]{:S(2)}) collective-permute-start(bf16[1,32,32,320]{3,2,1,0:T(8,128)(2,1)} %bitcast.32), channel_id=1, source_target_pairs={{0,1},{1,2},{2,3},{3,4},{4,5},{5,6},{6,7},{8,9},{9,10},{10,11},{11... | collective-permute-start | bytes 1966088 | tf_op jit(solution)/shard_map/ppermute | solution.py:19
  43.6 1.9 %collective-permute-start.3 = (bf16[1,32,32,320]{3,2,1,0:T(8,128)(2,1)}, bf16[1,32,32,320]{3,2,1,0:T(8,128)(2,1)}, u32[]{:S(2)}, u32[]{:S(2)}) collective-permute-start(bf16[1,32,32,320]{3,2,1,0:T(8,128)(2,1)} %bitcast.32), channel_id=1, source_target_pairs={{1,0},{2,1},{3,2},{4,3},{5,4},{6,5},{7,6},{9,8},{10,9},{11,10},{12... | collective-permute-start | bytes 1966088 | tf_op jit(solution)/shard_map/ppermute | solution.py:21
  45.7 0.2 convolution_reduce_fusion
  45.9 1.1 fusion.23
  46.9 1.5 %collective-permute-start.1 = (bf16[1,32,32,320]{3,2,1,0:T(8,128)(2,1)}, bf16[1,32,32,320]{3,2,1,0:T(8,128)(2,1)S(1)}, u32[]{:S(2)}, u32[]{:S(2)}) collective-permute-start(bf16[1,32,32,320]{3,2,1,0:T(8,128)(2,1)} %fusion.23), channel_id=1, source_target_pairs={{0,16},{8,24},{1,17},{9,25},{2,18},{10,26},{3,19},{11,27},{4,20},{... | collective-permute-start | bytes 1966088 | tf_op jit(solution)/shard_map/ppermute | solution.py:37
  48.4 1.8 %fusion.119 = f32[32,32,320]{2,1,0:T(8,128)S(1)} fusion(bf16[32,32,320]{2,1,0:T(8,128)(2,1)} %add_convert_fusion.2, bf16[3,320,320]{2,1,0:T(8,128)(2,1)S(1)} %copy-done.8), kind=kOutput, calls=%fused_computation.136 | convolution fusion | flops 209715200 | bytes 2211840 | tf_op jit(solution)/shard_map/dot_general | solution.py:81
  50.2 2.6 %collective-permute-done.2 = bf16[1,32,32,320]{3,2,1,0:T(8,128)(2,1)} collective-permute-done((bf16[1,32,32,320]{3,2,1,0:T(8,128)(2,1)}, bf16[1,32,32,320]{3,2,1,0:T(8,128)(2,1)}, u32[]{:S(2)}, u32[]{:S(2)}) %collective-permute-start.2) | collective-permute-done | bytes 655392 | tf_op jit(solution)/shard_map/ppermute | solution.py:19
  52.8 1.7 %fusion.92 = f32[32,32,320]{2,1,0:T(8,128)S(1)} fusion(bf16[1,32,32,320]{3,2,1,0:T(8,128)(2,1)} %collective-permute-done.2, bf16[3,320,320]{2,1,0:T(8,128)(2,1)S(1)} %copy-done.8), kind=kOutput, calls=%fused_computation.109 | convolution fusion | flops 209715200 | bytes 2211840 | tf_op jit(solution)/shard_map/dot_general | solution.py:81
  54.6 2.8 %collective-permute-done.3 = bf16[1,32,32,320]{3,2,1,0:T(8,128)(2,1)} collective-permute-done((bf16[1,32,32,320]{3,2,1,0:T(8,128)(2,1)}, bf16[1,32,32,320]{3,2,1,0:T(8,128)(2,1)}, u32[]{:S(2)}, u32[]{:S(2)}) %collective-permute-start.3) | collective-permute-done | bytes 655392 | tf_op jit(solution)/shard_map/ppermute | solution.py:21
  57.4 10.2 %collective-permute-done.1 = bf16[1,32,32,320]{3,2,1,0:T(8,128)(2,1)S(1)} collective-permute-done((bf16[1,32,32,320]{3,2,1,0:T(8,128)(2,1)}, bf16[1,32,32,320]{3,2,1,0:T(8,128)(2,1)S(1)}, u32[]{:S(2)}, u32[]{:S(2)}) %collective-permute-start.1) | collective-permute-done | bytes 655392 | tf_op jit(solution)/shard_map/ppermute | solution.py:37
  67.6 2.6 %convert_reduce_fusion.1 = (f32[320]{0:T(512)S(1)}, bf16[1,32,32,320]{3,2,1,0:T(8,128)(2,1)S(1)}) fusion(bf16[1,32,32,320]{3,2,1,0:T(8,128)(2,1)S(1)} %collective-permute-done.1, pred[]{:T(512)S(6)} %ne.9, bf16[1,32,32,320]{3,2,1,0:T(8,128)(2,1)S(1)} %collective-permute-done, pred[]{:T(512)S(6)} %ne.8, bf16[3,320,320]{2,1,0:T(8,128)(2,1)} %param.14, ...), kind=kOutput, calls=%fused_computation.9 | convolution fusion | flops 214957760 | bytes 6276354 | tf_op jit(solution)/shard_map/dot_general | solution.py:81
  70.3 0.1 reduce_sum.72
  70.5 0.1 sub.41
  70.6 0.3 fusion.13
  70.9 0.1 reduce_sum.74
  71.0 0.1 reduce_sum.75
  71.2 0.1 mul.159
  71.3 0.6 fusion.21
  71.9 1.7 %fusion.57 = f32[32,32,320]{2,1,0:T(8,128)S(1)} fusion(bf16[1,32,32,320]{3,2,1,0:T(8,128)(2,1)S(1)} %fusion.21, bf16[3,3,320,320]{3,2,1,0:T(8,128)(2,1)} %param.13), kind=kOutput, calls=%fused_computation.86 | convolution fusion | flops 209715200 | bytes 2211840 | tf_op jit(solution)/shard_map/dot_general | solution.py:71
  73.6 0.6 fusion.60
  74.2 0.6 fusion.63
  74.9 0.6 fusion.66
  75.5 0.6 fusion.69
  76.1 0.6 fusion.72
  76.8 0.6 fusion.75
  77.4 0.6 fusion.78
  78.0 1.2 multiply_convert_fusion
  79.2 4.2 %collective-permute-start.4 = (bf16[1,32,32,320]{3,2,1,0:T(8,128)(2,1)S(1)}, bf16[1,32,32,320]{3,2,1,0:T(8,128)(2,1)S(1)}, u32[]{:S(2)}, u32[]{:S(2)}) collective-permute-start(bf16[1,32,32,320]{3,2,1,0:T(8,128)(2,1)S(1)} %bitcast.208), channel_id=1, source_target_pairs={{0,1},{1,2},{2,3},{3,4},{4,5},{5,6},{6,7},{8,9},{9,10},{10,11},{11... | collective-permute-start | bytes 1966088 | tf_op jit(solution)/shard_map/ppermute | solution.py:19
  83.4 1.9 %collective-permute-start.5 = (bf16[1,32,32,320]{3,2,1,0:T(8,128)(2,1)S(1)}, bf16[1,32,32,320]{3,2,1,0:T(8,128)(2,1)S(1)}, u32[]{:S(2)}, u32[]{:S(2)}) collective-permute-start(bf16[1,32,32,320]{3,2,1,0:T(8,128)(2,1)S(1)} %bitcast.209), channel_id=1, source_target_pairs={{1,0},{2,1},{3,2},{4,3},{5,4},{6,5},{7,6},{9,8},{10,9},{11,10},{12... | collective-permute-start | bytes 1966088 | tf_op jit(solution)/shard_map/ppermute | solution.py:21
  85.3 0.6 fusion.117
  86.0 6.3 %collective-permute-done.4 = bf16[1,32,32,320]{3,2,1,0:T(8,128)(2,1)S(1)} collective-permute-done((bf16[1,32,32,320]{3,2,1,0:T(8,128)(2,1)S(1)}, bf16[1,32,32,320]{3,2,1,0:T(8,128)(2,1)S(1)}, u32[]{:S(2)}, u32[]{:S(2)}) %collective-permute-start.4) | collective-permute-done | bytes 655392 | tf_op jit(solution)/shard_map/ppermute | solution.py:19
  92.3 0.6 fusion.85
  92.9 3.8 %collective-permute-done.5 = bf16[1,32,32,320]{3,2,1,0:T(8,128)(2,1)S(1)} collective-permute-done((bf16[1,32,32,320]{3,2,1,0:T(8,128)(2,1)S(1)}, bf16[1,32,32,320]{3,2,1,0:T(8,128)(2,1)S(1)}, u32[]{:S(2)}, u32[]{:S(2)}) %collective-permute-start.5) | collective-permute-done | bytes 655392 | tf_op jit(solution)/shard_map/ppermute | solution.py:21
  96.7 0.6 add_convert_fusion
  97.4 1.3 collective-permute-start.6
  98.7 17.5 %collective-permute-done.6 = bf16[1,32,32,320]{3,2,1,0:T(8,128)(2,1)S(1)} collective-permute-done((bf16[1,32,32,320]{3,2,1,0:T(8,128)(2,1)S(1)}, bf16[1,32,32,320]{3,2,1,0:T(8,128)(2,1)S(1)}, u32[]{:S(2)}, u32[]{:S(2)}) %collective-permute-start.6) | collective-permute-done | bytes 655392 | tf_op jit(solution)/shard_map/ppermute | solution.py:37
  116.1 0.2 fusion.29
  116.4 1.3 collective-permute-start.7
  117.7 19.6 %collective-permute-done.7 = bf16[1,32,32,320]{3,2,1,0:T(8,128)(2,1)S(1)} collective-permute-done((bf16[1,32,32,320]{3,2,1,0:T(8,128)(2,1)S(1)}, bf16[1,32,32,320]{3,2,1,0:T(8,128)(2,1)S(1)}, u32[]{:S(2)}, u32[]{:S(2)}) %collective-permute-start.7) | collective-permute-done | bytes 655392 | tf_op jit(solution)/shard_map/ppermute | solution.py:37
  137.2 1.8 %fusion.96 = bf16[1,1,32,32,320]{4,3,2,1,0:T(8,128)(2,1)} fusion(bf16[1,32,32,320]{3,2,1,0:T(8,128)(2,1)S(1)} %collective-permute-done.7, bf16[1,32,32,320]{3,2,1,0:T(8,128)(2,1)S(1)} %collective-permute-done.6, bf16[1,1,32,32,320]{4,3,2,1,0:T(8,128)(2,1)S(1)} %copy-done.5, bf16[32,32,320]{2,1,0:T(8,128)(2,1)S(1)} %add_convert_fusion, ...), kind=kLoop, calls=%fused_computation.113 | loop fusion | flops 6225920 | bytes 5242882 | tf_op jit(solution)/shard_map/broadcast_in_dim | solution.py:120
  (55 shorter events, 1.2 us)
Async XLA Ops:
  0.0 28.7 %copy-start = (bf16[320,320]{1,0:T(8,128)(2,1)S(1)}, bf16[320,320]{1,0:T(8,128)(2,1)}, u32[]{:S(2)}) copy-start(bf16[320,320]{1,0:T(8,128)(2,1)} %param.15) | copy-start | bytes 614404
  0.0 3.9 %copy-start.1 = (bf16[1,32,32,320]{3,2,1,0:T(8,128)(2,1)S(1)}, bf16[1,32,32,320]{3,2,1,0:T(8,128)(2,1)}, u32[]{:S(2)}) copy-start(bf16[1,32,32,320]{3,2,1,0:T(8,128)(2,1)} %param.8) | copy-start | bytes 1966084
  0.0 3.9 %copy-start.11 = (f32[320]{0:T(512)S(1)}, f32[320]{0:T(512)}, u32[]{:S(2)}) copy-start(f32[320]{0:T(512)} %param.11) | copy-start | bytes 3844
  0.0 3.9 %copy-start.10 = (f32[320]{0:T(512)S(1)}, f32[320]{0:T(512)}, u32[]{:S(2)}) copy-start(f32[320]{0:T(512)} %param.12) | copy-start | bytes 3844
  0.0 45.8 %collective-permute-start = (bf16[1,32,32,320]{3,2,1,0:T(8,128)(2,1)}, bf16[1,32,32,320]{3,2,1,0:T(8,128)(2,1)S(1)}, u32[]{:S(2)}, u32[]{:S(2)}) collective-permute-start(bf16[1,32,32,320]{3,2,1,0:T(8,128)(2,1)} %bitcast.210), channel_id=1, source_target_pairs={{0,8},{8,0},{16,24},{24,16},{1,9},{9,1},{17,25},{25,17},{2,10},{10... | collective-permute-start | bytes 1966088 | tf_op jit(solution)/shard_map/ppermute | solution.py:37
  4.5 2.9 %copy-start.2 = (bf16[3,3,320,320]{3,2,1,0:T(8,128)(2,1)S(1)}, bf16[3,3,320,320]{3,2,1,0:T(8,128)(2,1)}, u32[]{:S(2)}) copy-start(bf16[3,3,320,320]{3,2,1,0:T(8,128)(2,1)} %param.13) | copy-start | bytes 5529604
  16.3 2.5 %copy-start.12 = (u32[32]{0:T(128)S(1)}, u32[32]{0:T(128)}, u32[]{:S(2)}) copy-start(u32[32]{0:T(128)} %constant.52) | copy-start | bytes 388
  30.8 15.1 %copy-start.4 = (bf16[1,1,32,32,320]{4,3,2,1,0:T(8,128)(2,1)S(1)}, bf16[1,1,32,32,320]{4,3,2,1,0:T(8,128)(2,1)}, u32[]{:S(2)}) copy-start(bf16[1,1,32,32,320]{4,3,2,1,0:T(8,128)(2,1)} %param.9) | copy-start | bytes 1966084
  37.4 11.1 %copy-start.8 = (bf16[3,320,320]{2,1,0:T(8,128)(2,1)S(1)}, bf16[3,320,320]{2,1,0:T(8,128)(2,1)}, u32[]{:S(2)}) copy-start(bf16[3,320,320]{2,1,0:T(8,128)(2,1)} %param.14) | copy-start | bytes 1843204
  37.4 15.4 %collective-permute-start.2 = (bf16[1,32,32,320]{3,2,1,0:T(8,128)(2,1)}, bf16[1,32,32,320]{3,2,1,0:T(8,128)(2,1)}, u32[]{:S(2)}, u32[]{:S(2)}) collective-permute-start(bf16[1,32,32,320]{3,2,1,0:T(8,128)(2,1)} %bitcast.32), channel_id=1, source_target_pairs={{0,1},{1,2},{2,3},{3,4},{4,5},{5,6},{6,7},{8,9},{9,10},{10,11},{11... | collective-permute-start | bytes 1966088 | tf_op jit(solution)/shard_map/ppermute | solution.py:19
  43.6 13.8 %collective-permute-start.3 = (bf16[1,32,32,320]{3,2,1,0:T(8,128)(2,1)}, bf16[1,32,32,320]{3,2,1,0:T(8,128)(2,1)}, u32[]{:S(2)}, u32[]{:S(2)}) collective-permute-start(bf16[1,32,32,320]{3,2,1,0:T(8,128)(2,1)} %bitcast.32), channel_id=1, source_target_pairs={{1,0},{2,1},{3,2},{4,3},{5,4},{6,5},{7,6},{9,8},{10,9},{11,10},{12... | collective-permute-start | bytes 1966088 | tf_op jit(solution)/shard_map/ppermute | solution.py:21
  46.9 20.6 %collective-permute-start.1 = (bf16[1,32,32,320]{3,2,1,0:T(8,128)(2,1)}, bf16[1,32,32,320]{3,2,1,0:T(8,128)(2,1)S(1)}, u32[]{:S(2)}, u32[]{:S(2)}) collective-permute-start(bf16[1,32,32,320]{3,2,1,0:T(8,128)(2,1)} %fusion.23), channel_id=1, source_target_pairs={{0,16},{8,24},{1,17},{9,25},{2,18},{10,26},{3,19},{11,27},{4,20},{... | collective-permute-start | bytes 1966088 | tf_op jit(solution)/shard_map/ppermute | solution.py:37
  67.6 2.6 %copy-start.6 = (bf16[1,32,32,320]{3,2,1,0:T(8,128)(2,1)}, bf16[1,32,32,320]{3,2,1,0:T(8,128)(2,1)S(1)}, u32[]{:S(2)}) copy-start(bf16[1,32,32,320]{3,2,1,0:T(8,128)(2,1)S(1)} %collective-permute-done.1) | copy-start | bytes 1966084
  71.9 1.7 %copy-start.3 = (bf16[3,3,320,320]{3,2,1,0:T(8,128)(2,1)S(1)}, bf16[3,3,320,320]{3,2,1,0:T(8,128)(2,1)}, u32[]{:S(2)}) copy-start(bf16[3,3,320,320]{3,2,1,0:T(8,128)(2,1)} %param.13) | copy-start | bytes 5529604
  78.0 7.3 %copy-start.9 = (bf16[3,320,320]{2,1,0:T(8,128)(2,1)S(1)}, bf16[3,320,320]{2,1,0:T(8,128)(2,1)}, u32[]{:S(2)}) copy-start(bf16[3,320,320]{2,1,0:T(8,128)(2,1)} %param.14) | copy-start | bytes 1843204
  79.2 13.1 %collective-permute-start.4 = (bf16[1,32,32,320]{3,2,1,0:T(8,128)(2,1)S(1)}, bf16[1,32,32,320]{3,2,1,0:T(8,128)(2,1)S(1)}, u32[]{:S(2)}, u32[]{:S(2)}) collective-permute-start(bf16[1,32,32,320]{3,2,1,0:T(8,128)(2,1)S(1)} %bitcast.208), channel_id=1, source_target_pairs={{0,1},{1,2},{2,3},{3,4},{4,5},{5,6},{6,7},{8,9},{9,10},{10,11},{11... | collective-permute-start | bytes 1966088 | tf_op jit(solution)/shard_map/ppermute | solution.py:19
  83.4 13.3 %collective-permute-start.5 = (bf16[1,32,32,320]{3,2,1,0:T(8,128)(2,1)S(1)}, bf16[1,32,32,320]{3,2,1,0:T(8,128)(2,1)S(1)}, u32[]{:S(2)}, u32[]{:S(2)}) collective-permute-start(bf16[1,32,32,320]{3,2,1,0:T(8,128)(2,1)S(1)} %bitcast.209), channel_id=1, source_target_pairs={{1,0},{2,1},{3,2},{4,3},{5,4},{6,5},{7,6},{9,8},{10,9},{11,10},{12... | collective-permute-start | bytes 1966088 | tf_op jit(solution)/shard_map/ppermute | solution.py:21
  97.4 39.9 %copy-start.5 = (bf16[1,1,32,32,320]{4,3,2,1,0:T(8,128)(2,1)S(1)}, bf16[1,1,32,32,320]{4,3,2,1,0:T(8,128)(2,1)}, u32[]{:S(2)}) copy-start(bf16[1,1,32,32,320]{4,3,2,1,0:T(8,128)(2,1)} %param.9) | copy-start | bytes 1966084
  97.4 39.9 %copy-start.7 = (bf16[1,32,32,320]{3,2,1,0:T(8,128)(2,1)S(1)}, bf16[1,32,32,320]{3,2,1,0:T(8,128)(2,1)}, u32[]{:S(2)}) copy-start(bf16[1,32,32,320]{3,2,1,0:T(8,128)(2,1)} %copy-done.6) | copy-start | bytes 1966084
  97.4 18.8 %collective-permute-start.6 = (bf16[1,32,32,320]{3,2,1,0:T(8,128)(2,1)S(1)}, bf16[1,32,32,320]{3,2,1,0:T(8,128)(2,1)S(1)}, u32[]{:S(2)}, u32[]{:S(2)}) collective-permute-start(bf16[1,32,32,320]{3,2,1,0:T(8,128)(2,1)S(1)} %bitcast.207), channel_id=1, source_target_pairs={{0,8},{8,0},{16,24},{24,16},{1,9},{9,1},{17,25},{25,17},{2,10},{10... | collective-permute-start | bytes 1966088 | tf_op jit(solution)/shard_map/ppermute | solution.py:37
  116.4 20.9 %collective-permute-start.7 = (bf16[1,32,32,320]{3,2,1,0:T(8,128)(2,1)S(1)}, bf16[1,32,32,320]{3,2,1,0:T(8,128)(2,1)S(1)}, u32[]{:S(2)}, u32[]{:S(2)}) collective-permute-start(bf16[1,32,32,320]{3,2,1,0:T(8,128)(2,1)S(1)} %fusion.29), channel_id=1, source_target_pairs={{0,16},{8,24},{1,17},{9,25},{2,18},{10,26},{3,19},{11,27},{4,20},{... | collective-permute-start | bytes 1966088 | tf_op jit(solution)/shard_map/ppermute | solution.py:37

commit v2 on v0

v2 whole, which is shorter than its diff:
```python
import functools
import math

import jax
import jax.numpy as jnp
from jax import lax
from jax.experimental import pallas as pl
from jax.experimental.pallas import tpu as pltpu
from jax.sharding import PartitionSpec as P

GROUPS = 32
CHUNKS = 4
MESH = pl.DeviceIdType.MESH
F32 = jnp.float32
BF16 = jnp.bfloat16


def silu(x):
    half = 0.5 * x
    return half + half * jnp.tanh(half)


def kernel(
    steps, frames, width,
    start, noise, when, gain, bias, sw, tw, tbw, out,
    tb_own, tb_all, same, x, state, act, act2, halo, upd, ntot, utot, nrecv, urecv,
    tb_send, tb_recv, h_send, h_recv, n_send, n_recv, u_send, u_recv,
):
    t = lax.axis_index("step")
    f = lax.axis_index("frame")
    cells, chan = start.shape
    size = cells // CHUNKS
    phases = len(range(0, steps.bit_length() - 1))
    has_left = f > 0
    has_right = f < frames - 1

    barrier = pltpu.get_barrier_semaphore()
    for d in range(1, steps):
        pl.semaphore_signal(barrier, inc=1, device_id=(lax.rem(t + d, steps), f), device_id_type=MESH)

    @pl.when(has_left)
    def _():
        pl.semaphore_signal(barrier, inc=1, device_id=(t, f - 1), device_id_type=MESH)

    @pl.when(has_right)
    def _():
        pl.semaphore_signal(barrier, inc=1, device_id=(t, f + 1), device_id_type=MESH)

    pl.semaphore_wait(barrier, steps - 1 + jnp.where(has_left, 1, 0) + jnp.where(has_right, 1, 0))

    def rows(c):
        return pl.ds(c * size, size)

    def bit(p):
        return lax.rem(t // (1 << p), 2)

    def swap(kind, p, c):
        own, tot, recv, ss, rs = (
            (noise, ntot, nrecv, n_send, n_recv) if kind == 0 else (upd, utot, urecv, u_send, u_recv)
        )
        src = own.at[rows(c)] if p == 0 else tot.at[p - 1, rows(c)]
        partner = t + (1 << p) * (1 - 2 * bit(p))
        return pltpu.make_async_remote_copy(
            src_ref=src, dst_ref=recv.at[p, rows(c)], send_sem=ss.at[p, c], recv_sem=rs.at[p, c],
            device_id=(partner, f), device_id_type=MESH,
        )

    def swap_do(kind, p, c, what):
        if p < phases - 1:
            what[0](swap(kind, p, c))
            return

        @pl.when(bit(p) == (0 if what[1] == "send" else 1))
        def _():
            what[0](swap(kind, p, c))

    begin = (lambda r: r.start(), "send")
    sent = (lambda r: r.wait_send(), "send")
    got = (lambda r: r.wait_recv(), "recv")

    def advance(kind, p, c):
        own, tot, recv = (noise, ntot, nrecv) if kind == 0 else (upd, utot, urecv)
        swap_do(kind, p, c, got)
        if p < phases - 1:
            have = own[rows(c), :] if p == 0 else tot[p - 1, rows(c), :]
            tot[p, rows(c), :] = (have.astype(F32) + recv[p, rows(c), :].astype(F32)).astype(BF16)
            swap_do(kind, p + 1, c, begin)

    def before(kind, c):
        recv = nrecv if kind == 0 else urecv
        total = jnp.zeros((size, chan), F32)
        for p in range(phases):
            total = total + jnp.where(bit(p) == 1, recv[p, rows(c), :].astype(F32), 0.0)
        return total

    def halo_copy(sweep, side, c):
        src = (act if sweep == 0 else act2).at[rows(c)]
        to = f + 1 if side == 0 else f - 1
        return pltpu.make_async_remote_copy(
            src_ref=src, dst_ref=halo.at[sweep, side, rows(c)],
            send_sem=h_send.at[sweep, side, c], recv_sem=h_recv.at[sweep, side, c],
            device_id=(t, to), device_id_type=MESH,
        )

    def halo_do(sweep, c, what):
        send = what[1] == "send"
        for side, cond in ((0, has_right if send else has_left), (1, has_left if send else has_right)):
            @pl.when(cond)
            def _():
                what[0](halo_copy(sweep, side, c))

    for c in range(CHUNKS):
        swap_do(0, 0, c, begin)

    lane = lax.broadcasted_iota(jnp.int32, (8, chan), 1)
    half = tbw.shape[0] // 2
    k = jnp.where(lane < half, lane, lane - half).astype(F32)
    angle = when[0].astype(F32) * jnp.exp(-math.log(10000.0) * k / half)
    emb = jnp.where(lane < half, jnp.cos(angle), jnp.sin(angle)).astype(BF16)
    tb_own[...] = silu(jnp.dot(emb, tbw[...], preferred_element_type=F32))

    def tb_copy(d):
        return pltpu.make_async_remote_copy(
            src_ref=tb_own, dst_ref=tb_all.at[d], send_sem=tb_send.at[d], recv_sem=tb_recv.at[d],
            device_id=(lax.rem(t + d, steps), f), device_id_type=MESH,
        )

    for d in range(1, steps):
        tb_copy(d).start()

    per = chan // GROUPS
    same[...] = jnp.where(
        lax.broadcasted_iota(jnp.int32, (chan, chan), 0) // per
        == lax.broadcasted_iota(jnp.int32, (chan, chan), 1) // per, 1.0, 0.0,
    ).astype(BF16)
    pad = jnp.zeros((width, x.shape[1]), BF16)
    x[pl.ds(0, width), :] = pad
    x[pl.ds(cells + width, width), :] = pad
    for sweep in range(2):
        @pl.when(jnp.logical_not(has_left))
        def _():
            halo[sweep, 0] = jnp.zeros((cells, chan), BF16)

        @pl.when(jnp.logical_not(has_right))
        def _():
            halo[sweep, 1] = jnp.zeros((cells, chan), BF16)

    @pl.when(bit(phases - 1) == 0)
    def _():
        nrecv[phases - 1] = jnp.zeros((cells, chan), BF16)
        urecv[phases - 1] = jnp.zeros((cells, chan), BF16)

    def group_mean(total):
        row = lax.broadcasted_iota(jnp.int32, (16, chan), 0)
        hi = total.astype(BF16).astype(F32)
        mid = (total - hi).astype(BF16).astype(F32)
        low = total - hi - mid
        parts = jnp.where(row == 0, hi, jnp.where(row == 1, mid, jnp.where(row == 2, low, 0.0)))
        summed = jnp.dot(parts.astype(BF16), same[...], preferred_element_type=F32)
        return jnp.sum(summed, axis=0, keepdims=True) / (per * cells)

    def fill(ref, total):
        mean = group_mean(total)
        var = jnp.zeros((1, chan), F32)
        for c in range(CHUNKS):
            centered = ref[rows(c), :].astype(F32) - mean
            var = var + jnp.sum(centered * centered, axis=0, keepdims=True)
        scale = lax.rsqrt(group_mean(var) + 1e-05) * gain[...]
        col = lax.rem(lax.broadcasted_iota(jnp.int32, (size, chan), 0), width)
        for c in range(CHUNKS):
            y = silu((ref[rows(c), :].astype(F32) - mean) * scale + bias[...])
            left = jnp.where(col == 0, 0.0, pltpu.roll(y, 1, 0))
            right = jnp.where(col == width - 1, 0.0, pltpu.roll(y, size - 1, 0))
            x[pl.ds(width + c * size, size), :] = jnp.concatenate([left, y, right], axis=1).astype(BF16)

    def conv(c):
        total = None
        for i in range(3):
            term = jnp.dot(x[pl.ds(c * size + i * width, size), :], sw[i], preferred_element_type=F32)
            total = term if total is None else total + term
        return total

    def temporal(sweep, c):
        halo_do(sweep, c, got)
        mine = act if sweep == 0 else act2
        total = jnp.dot(mine[rows(c), :], tw[1], preferred_element_type=F32)
        total = total + jnp.dot(halo[sweep, 0, rows(c), :], tw[0], preferred_element_type=F32)
        return total + jnp.dot(halo[sweep, 1, rows(c), :], tw[2], preferred_element_type=F32)

    total = jnp.zeros((1, chan), F32)
    for c in range(CHUNKS):
        total = total + jnp.sum(start[rows(c), :].astype(F32), axis=0, keepdims=True)
    fill(start, total)
    for d in range(1, steps):
        tb_copy(d).wait()
    for c in range(CHUNKS):
        acc = conv(c)
        summed = jnp.zeros_like(acc)
        for d in range(1, steps):
            summed = summed + jnp.where(d <= t, silu(acc + tb_all[d, 0:1, :]), 0.0)
        act[rows(c), :] = summed.astype(BF16)
        halo_do(0, c, begin)
        if c > 0:
            advance(0, 0, c - 1)
    advance(0, 0, CHUNKS - 1)
    for p in range(1, phases - 1):
        for c in range(CHUNKS):
            advance(0, p, c)
    total = jnp.zeros((1, chan), F32)
    for c in range(CHUNKS):
        update = temporal(0, c)
        if phases > 1:
            advance(0, phases - 1, c)
        now = (start[rows(c), :].astype(F32) + 0.25 * (update + before(0, c))).astype(BF16)
        state[rows(c), :] = now
        total = total + jnp.sum(now.astype(F32), axis=0, keepdims=True)

    fill(state, total)

    def second(c):
        upd[rows(c), :] = temporal(1, c).astype(BF16)
        swap_do(1, 0, c, begin)

    for c in range(CHUNKS):
        act2[rows(c), :] = silu(conv(c) + tb_own[0:1, :]).astype(BF16)
        halo_do(1, c, begin)
        if c > 1:
            second(c - 2)
    for c in range(CHUNKS - 2, CHUNKS):
        second(c)
        advance(1, 0, c - CHUNKS + 2)
    for c in range(2, CHUNKS):
        advance(1, 0, c)
    for p in range(1, phases - 1):
        for c in range(CHUNKS):
            advance(1, p, c)
    for c in range(CHUNKS):
        if phases > 1:
            advance(1, phases - 1, c)
        drift = before(0, c) + noise[rows(c), :].astype(F32) + before(1, c) + upd[rows(c), :].astype(F32)
        out[rows(c), :] = (start[rows(c), :].astype(F32) + 0.25 * drift).astype(BF16)

    for c in range(CHUNKS):
        for sweep in range(2):
            halo_do(sweep, c, sent)
        for kind in range(2):
            for p in range(phases):
                swap_do(kind, p, c, sent)


def local(steps, frames, start, noise, when, gain, bias, sw, tw, tbw):
    _, height, width, chan = start.shape
    cells = height * width
    phases = steps.bit_length() - 1
    big = (cells, chan)
    vm = pl.BlockSpec(memory_space=pltpu.VMEM)
    dma = pltpu.SemaphoreType.DMA
    out = pl.pallas_call(
        functools.partial(kernel, steps, frames, width),
        out_shape=jax.ShapeDtypeStruct(big, BF16),
        in_specs=[vm, vm, pl.BlockSpec(memory_space=pltpu.SMEM)] + [vm] * 5,
        out_specs=vm,
        scratch_shapes=[
            pltpu.VMEM((8, chan), F32),
            pltpu.VMEM((steps, 8, chan), F32),
            pltpu.VMEM((chan, chan), BF16),
            pltpu.VMEM((cells + 2 * width, 3 * chan), BF16),
            pltpu.VMEM(big, BF16),
            pltpu.VMEM(big, BF16),
            pltpu.VMEM(big, BF16),
            pltpu.VMEM((2, 2) + big, BF16),
            pltpu.VMEM(big, BF16),
            pltpu.VMEM((max(phases - 1, 1),) + big, BF16),
            pltpu.VMEM((max(phases - 1, 1),) + big, BF16),
            pltpu.VMEM((phases,) + big, BF16),
            pltpu.VMEM((phases,) + big, BF16),
            dma((steps,)), dma((steps,)),
            dma((2, 2, CHUNKS)), dma((2, 2, CHUNKS)),
            dma((phases, CHUNKS)), dma((phases, CHUNKS)),
            dma((phases, CHUNKS)), dma((phases, CHUNKS)),
        ],
        compiler_params=pltpu.CompilerParams(
            collective_id=0, has_side_effects=True, vmem_limit_bytes=48 * 1024 * 1024
        ),
    )(
        start.reshape(big), noise.reshape(big), when, gain.reshape(1, chan), bias.reshape(1, chan),
        sw.reshape(3, 3 * chan, chan), tw, tbw,
    )
    return out.reshape(1, 1, height, width, chan)


def solution(mesh):
    placed = (
        P("frame", None, None, None),
        P("step", "frame", None, None, None),
        P("step"),
        P(),
        P(),
        P(),
        P(),
        P(),
    )
    return jax.shard_map(
        functools.partial(local, mesh.shape["step"], mesh.shape["frame"]),
        mesh=mesh,
        in_specs=placed,
        out_specs=P("step", "frame", None, None, None),
        check_vma=False,
    )
```

time: 227 us -> 78.8 us (0.35)
  waiting for transfers between devices: 158 us -> 0 us
  Pallas kernels: 0 us -> 69.6 us
  other arithmetic: 22.1 us -> 0 us
  matrix products: 18.8 us -> 0 us
  between operations: 14.5 us -> 0.67 us
  starting transfers between devices: 11.4 us -> 0 us
  local copies, waits for them, and re-layouts: 1.54 us -> 8.2 us
    all_gather x2 -> x0, waiting for transfers between devices: 138 us -> none  [entering(): gathered = lax.all_gather(part, axis)]
    pallas_call x0 -> x1, Pallas kernels: none -> 69.6 us  [local(): pl.pallas_call(functools.partial(kernel, steps, frames, width), out_shape...]
    ppermute x4 -> x0, waiting for transfers between devices: 20.2 us -> none  [the longest x2 12.7 us: extended_2(): lax.ppermute(tail, axis, [(i, (i + 1) % count) for i in range(ends)])]
    dot_general x25 -> x0, matrix products: 18.8 us -> none  [the longest x18 12.3 us: spatial_conv(): jnp.dot(window, spatial_weight[row_off, col_off], preferred_element_type=...]
    ppermute x4 -> x0, starting transfers between devices: 11.3 us -> none  [the longest x2 7.43 us: extended_2(): lax.ppermute(tail, axis, [(i, (i + 1) % count) for i in range(ends)])]
    add x6 -> x0, other arithmetic: 10.9 us -> none  [combine_sum(): return earlier + later]
    unnamed x20 -> x11, local copies, waits for them, and re-layouts: 0.05 us -> 6.83 us
    reduce_sum x8 -> x0, other arithmetic: 6.09 us -> none  [the longest x4 3.26 us: norm_silu(): group_var = jnp.mean(centered * centered, axis=(1, 2, 4), keepdims=True)]
  transfers between devices with their start and end apart: 6 -> 0, of which waited for: 6 -> 0; matrix products, arithmetic and copies ran while one was open for 1% -> 0% of each run, Pallas kernels for 0% -> 0%
where the time goes in v2:
time: 78.8 us; the launch traced here: 78.4 us
  Pallas kernels  69.6 us (88%)
  local copies, waits for them, and re-layouts  8.2 us (10%)
    pallas_call x1, Pallas kernels, local(): pl.pallas_call(functools.partial(kernel, steps, frames, width), out_shape...  69.6 us
    unnamed x11, local copies, waits for them, and re-layouts  6.83 us

profile of v2, /device:TPU:23, one launch (start us, length us, event | category | flops | bytes accessed | tf_op | source)
XLA Modules:
  0.0 78.4 jit_solution(11211944954548700000)
XLA Ops:
  0.7 0.7 reshape.20.gain
  1.3 0.7 reshape.21.bias
  2.0 0.0 copy-start
  2.0 1.6 %copy-done = bf16[3,3,320,320]{3,2,1,0:T(8,128)(2,1)S(1)} copy-done((bf16[3,3,320,320]{3,2,1,0:T(8,128)(2,1)S(1)}, bf16[3,3,320,320]{3,2,1,0:T(8,128)(2,1)}, u32[]{:S(2)}) %copy-start) | copy-done | bytes 1843224
  3.6 0.0 copy-start.1
  3.6 1.1 %copy-done.1 = bf16[1,32,32,320]{3,2,1,0:T(8,128)(2,1)S(1)} copy-done((bf16[1,32,32,320]{3,2,1,0:T(8,128)(2,1)S(1)}, bf16[1,32,32,320]{3,2,1,0:T(8,128)(2,1)}, u32[]{:S(2)}) %copy-start.1) | copy-done | bytes 655384
  4.8 0.0 copy-start.2
  4.8 1.1 %copy-done.2 = bf16[1,1,32,32,320]{4,3,2,1,0:T(8,128)(2,1)S(1)} copy-done((bf16[1,1,32,32,320]{4,3,2,1,0:T(8,128)(2,1)S(1)}, bf16[1,1,32,32,320]{4,3,2,1,0:T(8,128)(2,1)}, u32[]{:S(2)}) %copy-start.2) | copy-done | bytes 655384
  5.9 0.0 copy-start.3
  5.9 1.1 %copy-done.3 = bf16[3,320,320]{2,1,0:T(8,128)(2,1)S(1)} copy-done((bf16[3,320,320]{2,1,0:T(8,128)(2,1)S(1)}, bf16[3,320,320]{2,1,0:T(8,128)(2,1)}, u32[]{:S(2)}) %copy-start.3) | copy-done | bytes 614424
  7.0 0.0 copy-start.4
  7.0 0.9 %copy-done.4 = bf16[320,320]{1,0:T(8,128)(2,1)S(1)} copy-done((bf16[320,320]{1,0:T(8,128)(2,1)S(1)}, bf16[320,320]{1,0:T(8,128)(2,1)}, u32[]{:S(2)}) %copy-start.4) | copy-done | bytes 204824
  8.0 69.6 %shard_map.82 = bf16[1024,320]{1,0:T(8,128)(2,1)S(1)} custom-call(bf16[1024,320]{1,0:T(8,128)(2,1)S(1)} %bitcast.6, bf16[1024,320]{1,0:T(8,128)(2,1)S(1)} %bitcast.7, s32[1]{0:T(128)S(6)} %copy.10.when, f32[1,320]{1,0:T(1,128)S(1)} %reshape.20.gain, f32[1,320]{1,0:T(1,128)S(1)} %reshape.21.bias, bf16[3,960,320]{2,1,0:T(8,128)(2,1)S(1)} %bitcast.5, ...), custom_call_target="tpu_custom_call" | custom-call | tf_op jit(solution)/shard_map/pallas_call | solution.py:258
  77.5 0.9 %copy.11 = bf16[1,1,32,32,320]{4,3,2,1,0:T(8,128)(2,1)} copy(bf16[1,1,32,32,320]{4,3,2,1,0:T(8,128)(2,1)S(1)} %bitcast.4) | data formatting | bytes 1310720
Async XLA Ops:
  2.0 1.6 %copy-start = (bf16[3,3,320,320]{3,2,1,0:T(8,128)(2,1)S(1)}, bf16[3,3,320,320]{3,2,1,0:T(8,128)(2,1)}, u32[]{:S(2)}) copy-start(bf16[3,3,320,320]{3,2,1,0:T(8,128)(2,1)} %param.13) | copy-start | bytes 5529604
  3.6 1.1 %copy-start.1 = (bf16[1,32,32,320]{3,2,1,0:T(8,128)(2,1)S(1)}, bf16[1,32,32,320]{3,2,1,0:T(8,128)(2,1)}, u32[]{:S(2)}) copy-start(bf16[1,32,32,320]{3,2,1,0:T(8,128)(2,1)} %param.8) | copy-start | bytes 1966084
  4.8 1.1 %copy-start.2 = (bf16[1,1,32,32,320]{4,3,2,1,0:T(8,128)(2,1)S(1)}, bf16[1,1,32,32,320]{4,3,2,1,0:T(8,128)(2,1)}, u32[]{:S(2)}) copy-start(bf16[1,1,32,32,320]{4,3,2,1,0:T(8,128)(2,1)} %param.9) | copy-start | bytes 1966084
  5.9 1.1 %copy-start.3 = (bf16[3,320,320]{2,1,0:T(8,128)(2,1)S(1)}, bf16[3,320,320]{2,1,0:T(8,128)(2,1)}, u32[]{:S(2)}) copy-start(bf16[3,320,320]{2,1,0:T(8,128)(2,1)} %tw.1) | copy-start | bytes 1843204
  7.0 0.9 %copy-start.4 = (bf16[320,320]{1,0:T(8,128)(2,1)S(1)}, bf16[320,320]{1,0:T(8,128)(2,1)}, u32[]{:S(2)}) copy-start(bf16[320,320]{1,0:T(8,128)(2,1)} %tbw.1) | copy-start | bytes 614404

commit v3 on v2

--- a/solution.py
+++ b/solution.py
@@ -10,6 +10,7 @@
 
 GROUPS = 32
 CHUNKS = 4
+LANES = 128
 MESH = pl.DeviceIdType.MESH
 F32 = jnp.float32
 BF16 = jnp.bfloat16
@@ -20,11 +21,33 @@
     return half + half * jnp.tanh(half)
 
 
+def pack(v):
+    n, c = v.shape
+    full = c // LANES * LANES
+    rest = c - full
+    if not rest:
+        return v.astype(BF16)
+    q = n * rest // full
+    tail = jnp.concatenate([v[i * q : (i + 1) * q, full:] for i in range(n // q)], axis=1)
+    return jnp.concatenate([v[:, :full], tail], axis=0).astype(BF16)
+
+
+def unpack(w, n, c):
+    full = w.shape[1]
+    rest = c - full
+    w = w.astype(F32)
+    if not rest:
+        return w
+    tail = jnp.concatenate([w[n:, i * rest : (i + 1) * rest] for i in range(full // rest)], axis=0)
+    return jnp.concatenate([w[:n], tail], axis=1)
+
+
 def kernel(
     steps, frames, width,
-    start, noise, when, gain, bias, sw, tw, tbw, out,
-    tb_own, tb_all, same, x, state, act, act2, halo, upd, ntot, utot, nrecv, urecv,
-    tb_send, tb_recv, h_send, h_recv, n_send, n_recv, u_send, u_recv,
+    start_in, noise_in, when, gain, bias, sw_in, tw_in, tbw_in, out,
+    start, noise, sw, tw, tbw,
+    tb_own, tb_all, same, x, state, act, noise_p, act_p, halo, upd, upd_p, ntot, utot, nrecv, urecv,
+    load_sem, tb_send, tb_recv, h_send, h_recv, n_send, n_recv, u_send, u_recv,
 ):
     t = lax.axis_index("step")
     f = lax.axis_index("frame")
@@ -34,6 +57,15 @@
     has_left = f > 0
     has_right = f < frames - 1
 
+    loads = [
+        pltpu.make_async_copy(src, dst, load_sem.at[i])
+        for i, (src, dst) in enumerate(
+            [(noise_in, noise), (start_in, start), (tbw_in, tbw), (sw_in, sw), (tw_in, tw)]
+        )
+    ]
+    for load in loads:
+        load.start()
+
     barrier = pltpu.get_barrier_semaphore()
     for d in range(1, steps):
         pl.semaphore_signal(barrier, inc=1, device_id=(lax.rem(t + d, steps), f), device_id_type=MESH)
@@ -51,17 +83,22 @@
     def rows(c):
         return pl.ds(c * size, size)
 
+    packed = noise_p.shape[0] // CHUNKS
+
+    def prows(c):
+        return pl.ds(c * packed, packed)
+
     def bit(p):
         return lax.rem(t // (1 << p), 2)
 
     def swap(kind, p, c):
         own, tot, recv, ss, rs = (
-            (noise, ntot, nrecv, n_send, n_recv) if kind == 0 else (upd, utot, urecv, u_send, u_recv)
-        )
-        src = own.at[rows(c)] if p == 0 else tot.at[p - 1, rows(c)]
+            (noise_p, ntot, nrecv, n_send, n_recv) if kind == 0 else (upd_p, utot, urecv, u_send, u_recv)
+        )
+        src = own.at[prows(c)] if p == 0 else tot.at[p - 1, prows(c)]
         partner = t + (1 << p) * (1 - 2 * bit(p))
         return pltpu.make_async_remote_copy(
-            src_ref=src, dst_ref=recv.at[p, rows(c)], send_sem=ss.at[p, c], recv_sem=rs.at[p, c],
+            src_ref=src, dst_ref=recv.at[p, prows(c)], send_sem=ss.at[p, c], recv_sem=rs.at[p, c],
             device_id=(partner, f), device_id_type=MESH,
         )
 
@@ -79,25 +116,24 @@
     got = (lambda r: r.wait_recv(), "recv")
 
     def advance(kind, p, c):
-        own, tot, recv = (noise, ntot, nrecv) if kind == 0 else (upd, utot, urecv)
+        own, tot, recv = (noise_p, ntot, nrecv) if kind == 0 else (upd_p, utot, urecv)
         swap_do(kind, p, c, got)
         if p < phases - 1:
-            have = own[rows(c), :] if p == 0 else tot[p - 1, rows(c), :]
-            tot[p, rows(c), :] = (have.astype(F32) + recv[p, rows(c), :].astype(F32)).astype(BF16)
+            have = own[prows(c), :] if p == 0 else tot[p - 1, prows(c), :]
+            tot[p, prows(c), :] = (have.astype(F32) + recv[p, prows(c), :].astype(F32)).astype(BF16)
             swap_do(kind, p + 1, c, begin)
 
-    def before(kind, c):
-        recv = nrecv if kind == 0 else urecv
-        total = jnp.zeros((size, chan), F32)
-        for p in range(phases):
-            total = total + jnp.where(bit(p) == 1, recv[p, rows(c), :].astype(F32), 0.0)
-        return total
+    def before(c, *recvs):
+        total = jnp.zeros((packed, noise_p.shape[1]), F32)
+        for recv in recvs:
+            for p in range(phases):
+                total = total + jnp.where(bit(p) == 1, recv[p, prows(c), :].astype(F32), 0.0)
+        return unpack(total, size, chan)
 
     def halo_copy(sweep, side, c):
-        src = (act if sweep == 0 else act2).at[rows(c)]
         to = f + 1 if side == 0 else f - 1
         return pltpu.make_async_remote_copy(
-            src_ref=src, dst_ref=halo.at[sweep, side, rows(c)],
+            src_ref=act_p.at[sweep, prows(c)], dst_ref=halo.at[sweep, side, prows(c)],
             send_sem=h_send.at[sweep, side, c], recv_sem=h_recv.at[sweep, side, c],
             device_id=(t, to), device_id_type=MESH,
         )
@@ -109,9 +145,12 @@
             def _():
                 what[0](halo_copy(sweep, side, c))
 
-    for c in range(CHUNKS):
+    loads[0].wait()
+    for c in range(CHUNKS):
+        noise_p[prows(c), :] = pack(noise[rows(c), :].astype(F32))
         swap_do(0, 0, c, begin)
 
+    loads[2].wait()
     lane = lax.broadcasted_iota(jnp.int32, (8, chan), 1)
     half = tbw.shape[0] // 2
     k = jnp.where(lane < half, lane, lane - half).astype(F32)
@@ -139,16 +178,16 @@
     for sweep in range(2):
         @pl.when(jnp.logical_not(has_left))
         def _():
-            halo[sweep, 0] = jnp.zeros((cells, chan), BF16)
+            halo[sweep, 0] = jnp.zeros(noise_p.shape, BF16)
 
         @pl.when(jnp.logical_not(has_right))
         def _():
-            halo[sweep, 1] = jnp.zeros((cells, chan), BF16)
+            halo[sweep, 1] = jnp.zeros(noise_p.shape, BF16)
 
     @pl.when(bit(phases - 1) == 0)
     def _():
-        nrecv[phases - 1] = jnp.zeros((cells, chan), BF16)
-        urecv[phases - 1] = jnp.zeros((cells, chan), BF16)
+        nrecv[phases - 1] = jnp.zeros(noise_p.shape, BF16)
+        urecv[phases - 1] = jnp.zeros(noise_p.shape, BF16)
 
     def group_mean(total):
         row = lax.broadcasted_iota(jnp.int32, (16, chan), 0)
@@ -165,10 +204,10 @@
         for c in range(CHUNKS):
             centered = ref[rows(c), :].astype(F32) - mean
             var = var + jnp.sum(centered * centered, axis=0, keepdims=True)
-        scale = lax.rsqrt(group_mean(var) + 1e-05) * gain[...]
+        scale = lax.rsqrt(group_mean(var) + 1e-05) * gain[...].reshape(1, chan)
         col = lax.rem(lax.broadcasted_iota(jnp.int32, (size, chan), 0), width)
         for c in range(CHUNKS):
-            y = silu((ref[rows(c), :].astype(F32) - mean) * scale + bias[...])
+            y = silu((ref[rows(c), :].astype(F32) - mean) * scale + bias[...].reshape(1, chan))
             left = jnp.where(col == 0, 0.0, pltpu.roll(y, 1, 0))
             right = jnp.where(col == width - 1, 0.0, pltpu.roll(y, size - 1, 0))
             x[pl.ds(width + c * size, size), :] = jnp.concatenate([left, y, right], axis=1).astype(BF16)
@@ -182,23 +221,27 @@
 
     def temporal(sweep, c):
         halo_do(sweep, c, got)
-        mine = act if sweep == 0 else act2
-        total = jnp.dot(mine[rows(c), :], tw[1], preferred_element_type=F32)
-        total = total + jnp.dot(halo[sweep, 0, rows(c), :], tw[0], preferred_element_type=F32)
-        return total + jnp.dot(halo[sweep, 1, rows(c), :], tw[2], preferred_element_type=F32)
-
+        total = jnp.dot(act[sweep, rows(c), :], tw[1], preferred_element_type=F32)
+        for side in range(2):
+            beside = unpack(halo[sweep, side, prows(c), :], size, chan).astype(BF16)
+            total = total + jnp.dot(beside, tw[2 * side], preferred_element_type=F32)
+        return total
+
+    loads[1].wait()
     total = jnp.zeros((1, chan), F32)
     for c in range(CHUNKS):
         total = total + jnp.sum(start[rows(c), :].astype(F32), axis=0, keepdims=True)
     fill(start, total)
     for d in range(1, steps):
         tb_copy(d).wait()
+    loads[3].wait()
     for c in range(CHUNKS):
         acc = conv(c)
         summed = jnp.zeros_like(acc)
         for d in range(1, steps):
             summed = summed + jnp.where(d <= t, silu(acc + tb_all[d, 0:1, :]), 0.0)
-        act[rows(c), :] = summed.astype(BF16)
+        act[0, rows(c), :] = summed.astype(BF16)
+        act_p[0, prows(c), :] = pack(summed)
         halo_do(0, c, begin)
         if c > 0:
             advance(0, 0, c - 1)
@@ -206,23 +249,28 @@
     for p in range(1, phases - 1):
         for c in range(CHUNKS):
             advance(0, p, c)
+    loads[4].wait()
     total = jnp.zeros((1, chan), F32)
     for c in range(CHUNKS):
         update = temporal(0, c)
         if phases > 1:
             advance(0, phases - 1, c)
-        now = (start[rows(c), :].astype(F32) + 0.25 * (update + before(0, c))).astype(BF16)
+        now = (start[rows(c), :].astype(F32) + 0.25 * (update + before(c, nrecv))).astype(BF16)
         state[rows(c), :] = now
         total = total + jnp.sum(now.astype(F32), axis=0, keepdims=True)
 
     fill(state, total)
 
     def second(c):
-        upd[rows(c), :] = temporal(1, c).astype(BF16)
+        update = temporal(1, c)
+        upd_p[prows(c), :] = pack(update)
+        upd[rows(c), :] = (update + noise[rows(c), :].astype(F32)) * 0.25 + start[rows(c), :].astype(F32)
         swap_do(1, 0, c, begin)
 
     for c in range(CHUNKS):
-        act2[rows(c), :] = silu(conv(c) + tb_own[0:1, :]).astype(BF16)
+        active = silu(conv(c) + tb_own[0:1, :])
+        act[1, rows(c), :] = active.astype(BF16)
+        act_p[1, prows(c), :] = pack(active)
         halo_do(1, c, begin)
         if c > 1:
             second(c - 2)
@@ -237,8 +285,7 @@
     for c in range(CHUNKS):
         if phases > 1:
             advance(1, phases - 1, c)
-        drift = before(0, c) + noise[rows(c), :].astype(F32) + before(1, c) + upd[rows(c), :].astype(F32)
-        out[rows(c), :] = (start[rows(c), :].astype(F32) + 0.25 * drift).astype(BF16)
+        out[rows(c), :] = (upd[rows(c), :] + 0.25 * before(c, nrecv, urecv)).astype(BF16)
 
     for c in range(CHUNKS):
         for sweep in range(2):
@@ -253,27 +300,38 @@
     cells = height * width
     phases = steps.bit_length() - 1
     big = (cells, chan)
+    full = chan // LANES * LANES
+    small = (cells * chan // full, full)
+    hbm = pl.BlockSpec(memory_space=pltpu.HBM)
     vm = pl.BlockSpec(memory_space=pltpu.VMEM)
     dma = pltpu.SemaphoreType.DMA
     out = pl.pallas_call(
         functools.partial(kernel, steps, frames, width),
         out_shape=jax.ShapeDtypeStruct(big, BF16),
-        in_specs=[vm, vm, pl.BlockSpec(memory_space=pltpu.SMEM)] + [vm] * 5,
+        in_specs=[hbm, hbm, pl.BlockSpec(memory_space=pltpu.SMEM), vm, vm, hbm, hbm, hbm],
         out_specs=vm,
         scratch_shapes=[
+            pltpu.VMEM(big, BF16),
+            pltpu.VMEM(big, BF16),
+            pltpu.VMEM((3, 3 * chan, chan), BF16),
+            pltpu.VMEM(tw.shape, BF16),
+            pltpu.VMEM(tbw.shape, BF16),
             pltpu.VMEM((8, chan), F32),
             pltpu.VMEM((steps, 8, chan), F32),
             pltpu.VMEM((chan, chan), BF16),
             pltpu.VMEM((cells + 2 * width, 3 * chan), BF16),
             pltpu.VMEM(big, BF16),
-            pltpu.VMEM(big, BF16),
-            pltpu.VMEM(big, BF16),
-            pltpu.VMEM((2, 2) + big, BF16),
-            pltpu.VMEM(big, BF16),
-            pltpu.VMEM((max(phases - 1, 1),) + big, BF16),
-            pltpu.VMEM((max(phases - 1, 1),) + big, BF16),
-            pltpu.VMEM((phases,) + big, BF16),
-            pltpu.VMEM((phases,) + big, BF16),
+            pltpu.VMEM((2,) + big, BF16),
+            pltpu.VMEM(small, BF16),
+            pltpu.VMEM((2,) + small, BF16),
+            pltpu.VMEM((2, 2) + small, BF16),
+            pltpu.VMEM(big, F32),
+            pltpu.VMEM(small, BF16),
+            pltpu.VMEM((max(phases - 1, 1),) + small, BF16),
+            pltpu.VMEM((max(phases - 1, 1),) + small, BF16),
+            pltpu.VMEM((phases,) + small, BF16),
+            pltpu.VMEM((phases,) + small, BF16),
+            dma((5,)),
             dma((steps,)), dma((steps,)),
             dma((2, 2, CHUNKS)), dma((2, 2, CHUNKS)),
             dma((phases, CHUNKS)), dma((phases, CHUNKS)),
@@ -283,7 +341,7 @@
             collective_id=0, has_side_effects=True, vmem_limit_bytes=48 * 1024 * 1024
         ),
     )(
-        start.reshape(big), noise.reshape(big), when, gain.reshape(1, chan), bias.reshape(1, chan),
+        start.reshape(big), noise.reshape(big), when, gain, bias,
         sw.reshape(3, 3 * chan, chan), tw, tbw,
     )
     return out.reshape(1, 1, height, width, chan)

time: 78.8 us -> 71 us (0.901)
  Pallas kernels: 69.6 us -> 61.8 us
    pallas_call x1, Pallas kernels: 69.6 us -> 61.8 us  [local(): pl.pallas_call(functools.partial(kernel, steps, frames, width), out_shape...]
    reshape x2 -> x0, local copies, waits for them, and re-layouts: 1.37 us -> none  [the longest x1 0.68 us: local(): gain.reshape(1, chan)]
    unnamed x11 -> x15, local copies, waits for them, and re-layouts: 6.83 us -> 8.19 us
where the time goes in v3:
time: 71 us; the launch traced here: 70.7 us
  Pallas kernels  61.8 us (87%)
  local copies, waits for them, and re-layouts  8.19 us (12%)
    pallas_call x1, Pallas kernels, local(): pl.pallas_call(functools.partial(kernel, steps, frames, width), out_shape...  61.8 us
    unnamed x15, local copies, waits for them, and re-layouts  8.19 us

profile of v3, /device:TPU:23, one launch (start us, length us, event | category | flops | bytes accessed | tf_op | source)
XLA Modules:
  0.0 70.7 jit_solution(10103580176502484306)
XLA Ops:
  0.7 0.0 copy-start
  0.7 1.6 %copy-done = bf16[3,3,320,320]{3,2,1,0:T(8,128)(2,1)S(1)} copy-done((bf16[3,3,320,320]{3,2,1,0:T(8,128)(2,1)S(1)}, bf16[3,3,320,320]{3,2,1,0:T(8,128)(2,1)}, u32[]{:S(2)}) %copy-start) | copy-done | bytes 1843224
  2.3 0.0 copy-start.1
  2.3 1.1 %copy-done.1 = bf16[1,32,32,320]{3,2,1,0:T(8,128)(2,1)S(1)} copy-done((bf16[1,32,32,320]{3,2,1,0:T(8,128)(2,1)S(1)}, bf16[1,32,32,320]{3,2,1,0:T(8,128)(2,1)}, u32[]{:S(2)}) %copy-start.1) | copy-done | bytes 655384
  3.4 0.0 copy-start.2
  3.4 1.1 %copy-done.2 = bf16[1,1,32,32,320]{4,3,2,1,0:T(8,128)(2,1)S(1)} copy-done((bf16[1,1,32,32,320]{4,3,2,1,0:T(8,128)(2,1)S(1)}, bf16[1,1,32,32,320]{4,3,2,1,0:T(8,128)(2,1)}, u32[]{:S(2)}) %copy-start.2) | copy-done | bytes 655384
  4.5 0.0 copy-start.3
  4.5 1.1 %copy-done.3 = bf16[3,320,320]{2,1,0:T(8,128)(2,1)S(1)} copy-done((bf16[3,320,320]{2,1,0:T(8,128)(2,1)S(1)}, bf16[3,320,320]{2,1,0:T(8,128)(2,1)}, u32[]{:S(2)}) %copy-start.3) | copy-done | bytes 614424
  5.7 0.0 copy-start.4
  5.7 0.9 %copy-done.4 = bf16[320,320]{1,0:T(8,128)(2,1)S(1)} copy-done((bf16[320,320]{1,0:T(8,128)(2,1)S(1)}, bf16[320,320]{1,0:T(8,128)(2,1)}, u32[]{:S(2)}) %copy-start.4) | copy-done | bytes 204824
  6.6 0.0 copy-start.5
  6.6 0.7 copy-done.5
  7.3 0.0 copy-start.6
  7.3 0.7 copy-done.6
  8.0 61.8 %shard_map.82 = bf16[1024,320]{1,0:T(8,128)(2,1)S(1)} custom-call(bf16[1024,320]{1,0:T(8,128)(2,1)S(1)} %bitcast.6, bf16[1024,320]{1,0:T(8,128)(2,1)S(1)} %bitcast.7, s32[1]{0:T(128)S(6)} %copy.10.when, f32[320]{0:T(512)S(1)} %copy-done.5, f32[320]{0:T(512)S(1)} %copy-done.6, bf16[3,960,320]{2,1,0:T(8,128)(2,1)S(1)} %bitcast.5, ...), custom_call_target="tpu_custom_call" | custom-call | tf_op jit(solution)/shard_map/pallas_call | solution.py:308
  69.8 0.9 %copy.11 = bf16[1,1,32,32,320]{4,3,2,1,0:T(8,128)(2,1)} copy(bf16[1,1,32,32,320]{4,3,2,1,0:T(8,128)(2,1)S(1)} %bitcast.4) | data formatting | bytes 1310720
Async XLA Ops:
  0.7 1.6 %copy-start = (bf16[3,3,320,320]{3,2,1,0:T(8,128)(2,1)S(1)}, bf16[3,3,320,320]{3,2,1,0:T(8,128)(2,1)}, u32[]{:S(2)}) copy-start(bf16[3,3,320,320]{3,2,1,0:T(8,128)(2,1)} %param.13) | copy-start | bytes 5529604
  2.3 1.1 %copy-start.1 = (bf16[1,32,32,320]{3,2,1,0:T(8,128)(2,1)S(1)}, bf16[1,32,32,320]{3,2,1,0:T(8,128)(2,1)}, u32[]{:S(2)}) copy-start(bf16[1,32,32,320]{3,2,1,0:T(8,128)(2,1)} %param.8) | copy-start | bytes 1966084
  3.4 1.1 %copy-start.2 = (bf16[1,1,32,32,320]{4,3,2,1,0:T(8,128)(2,1)S(1)}, bf16[1,1,32,32,320]{4,3,2,1,0:T(8,128)(2,1)}, u32[]{:S(2)}) copy-start(bf16[1,1,32,32,320]{4,3,2,1,0:T(8,128)(2,1)} %param.9) | copy-start | bytes 1966084
  4.5 1.1 %copy-start.3 = (bf16[3,320,320]{2,1,0:T(8,128)(2,1)S(1)}, bf16[3,320,320]{2,1,0:T(8,128)(2,1)}, u32[]{:S(2)}) copy-start(bf16[3,320,320]{2,1,0:T(8,128)(2,1)} %tw_in.1) | copy-start | bytes 1843204
  5.7 0.9 %copy-start.4 = (bf16[320,320]{1,0:T(8,128)(2,1)S(1)}, bf16[320,320]{1,0:T(8,128)(2,1)}, u32[]{:S(2)}) copy-start(bf16[320,320]{1,0:T(8,128)(2,1)} %tbw_in.1) | copy-start | bytes 614404
  6.6 0.7 copy-start.5
  7.3 0.7 copy-start.6
